TPU v7x, 32 devices: a whole 2x2x4 slice. The times are simulated.
32 devices in a mesh: seq: 8 (over z, core), tp: 4 (over y, x).
Axes of the slice: x: 2, y: 2, z: 4, core: 2. Of those that a mesh axis runs over, the one named last changes fastest.
Arguments:
- queries: bfloat16 [4096, 6144], P(('seq', 'tp')), may hold values from -6 to 6
- keys: bfloat16 [4096, 6144], P(('seq', 'tp')), may hold values from -1.25 to 1.25
- values: bfloat16 [4096, 6144], P(('seq', 'tp')), may hold values from -6 to 6
- decay_rates: float32 [48], P('tp'), may hold values from 1e-05 to 0.03
- norm_gain: float32 [6144], P('tp'), may hold values from 0.25 to 1.75
- out_weight: bfloat16 [6144, 6144], P('tp'), may hold values from -0.078125 to 0.078125
- doc_lengths: int32 [32], replicated, may hold values from 1 to 2048, 4096 in all
Outputs:
- mixed: bfloat16 [4096, 6144], P(('seq', 'tp'))
All inputs are finite; a program needn't handle non-finite values.
Results may differ from a plain program's by a relative error of at most 0.014.
Values may be sent and summed in bfloat16 or wider, within the bound.
A program may use at most 128 MiB of HBM per device.

v0:
```python
import jax
import jax.numpy as jnp
from jax import lax
from jax.sharding import PartitionSpec as P


def carried_in(x, axis, combine, identity):
    count, position = (lax.axis_size(axis), lax.axis_index(axis))
    everything = jax.tree.map(
        lambda part, kind: lax.all_gather(part.astype(kind), axis), x, (jnp.bfloat16, jnp.bfloat16)
    )
    start = jax.tree.map(
        lambda part, zero: jnp.broadcast_to(jnp.asarray(zero, part.dtype), part.shape), x, identity
    )

    def step(k, before):
        reached = k < position
        new = combine(
            before, jax.tree.map(lambda part, own: part[k].astype(own.dtype), everything, x)
        )
        return jax.tree.map(lambda a, b: jnp.where(reached, a, b), new, before)

    return lax.fori_loop(0, count, step, start)


def segment_ids(positions, doc_ends):
    return jnp.sum((doc_ends[None, :] <= positions[:, None]).astype(jnp.int32), axis=1)


def local_pass(q_heads, k_heads, v_heads, segments, decay_rates, seg_start):
    highest = lax.Precision.HIGHEST
    total_rows, heads_dev, head_dim = q_heads.shape
    block_rows = min(256, total_rows)
    block_count = total_rows // block_rows
    shape_four = (block_count, block_rows, heads_dev, head_dim)
    q_blocks = q_heads.reshape(shape_four)
    k_blocks = k_heads.reshape(shape_four)
    v_blocks = v_heads.reshape(shape_four)
    seg_blocks = segments.reshape(block_count, block_rows)
    offsets = jnp.arange(block_rows).astype(jnp.float32)
    distance = offsets[:, None] - offsets[None, :]
    causal = distance >= 0
    base_decay = jnp.exp(-decay_rates[:, None, None] * jnp.maximum(distance, 0.0)[None])
    allowed = causal[None] & (seg_blocks[:, :, None] == seg_blocks[:, None, :])
    decay_mat = jnp.where(allowed[:, None], base_decay[None], 0.0)
    scores = jnp.einsum("bthd,bshd->bhts", q_blocks, k_blocks, preferred_element_type=jnp.float32)
    weighted = (scores * decay_mat).astype(jnp.bfloat16)
    inside = jnp.einsum("bhts,bshd->bthd", weighted, v_blocks, preferred_element_type=jnp.float32)
    last_segs = seg_blocks[:, -1]
    prev_segs = jnp.concatenate([jnp.reshape(seg_start, (1,)), last_segs[:-1]])
    carry_in = jnp.where(
        (seg_blocks == prev_segs[:, None])[:, :, None],
        jnp.exp(-decay_rates[None, :] * (offsets + 1.0)[:, None])[None],
        0.0,
    )
    keep_end = jnp.where(
        (seg_blocks == last_segs[:, None])[:, :, None],
        jnp.exp(-decay_rates[None, :] * (block_rows - 1.0 - offsets)[:, None])[None],
        0.0,
    )
    whole_keep = jnp.where(
        (last_segs == prev_segs)[:, None], jnp.exp(-decay_rates * block_rows)[None, :], 0.0
    )
    weighted_keys = (k_blocks.astype(jnp.float32) * keep_end[:, :, :, None]).astype(jnp.bfloat16)
    local_states = jnp.einsum(
        "bshd,bshe->bhde", weighted_keys, v_blocks, preferred_element_type=jnp.float32
    )

    def advance(running, pieces):
        kv_state, decay_total = running
        keep_now, state_now = pieces
        following = keep_now[:, None, None] * kv_state + state_now
        return ((following, decay_total * keep_now), kv_state)

    initial = (
        jnp.zeros((heads_dev, head_dim, head_dim), jnp.float32),
        jnp.ones((heads_dev,), jnp.float32),
    )
    finished, entering = lax.scan(advance, initial, (whole_keep, local_states))
    carried = jnp.einsum(
        "bthd,bhde->bthe", q_blocks.astype(jnp.float32), entering, precision=highest
    )
    attended = inside + carried * carry_in[:, :, :, None]
    return (attended.reshape(total_rows, heads_dev, head_dim), finished[0], finished[1])


def combine_states(earlier, later):
    return (earlier[0] * later[0], later[0][:, None, None] * earlier[1] + later[1])


def local(queries, keys, values, decay_rates, norm_gain, out_weight, doc_lengths):
    highest = lax.Precision.HIGHEST
    q_heads, k_heads, v_heads = (
        lax.all_to_all(queries, "tp", split_axis=1, concat_axis=0, tiled=True),
        lax.all_to_all(keys, "tp", split_axis=1, concat_axis=0, tiled=True),
        lax.all_to_all(values, "tp", split_axis=1, concat_axis=0, tiled=True),
    )
    heads_dev = decay_rates.shape[0]
    seq_rows = q_heads.shape[0]
    head_dim = q_heads.shape[1] // heads_dev
    group_size = lax.axis_size("tp")
    first_row = lax.axis_index("seq") * seq_rows
    doc_ends = jnp.cumsum(doc_lengths)
    positions = first_row + jnp.arange(seq_rows, dtype=jnp.int32)
    segments = segment_ids(positions, doc_ends)
    seg_before = segment_ids(jnp.reshape(first_row - 1, (1,)), doc_ends)[0]
    shaped = (seq_rows, heads_dev, head_dim)
    attended, kv_state, decay_total = local_pass(
        q_heads.reshape(shaped),
        k_heads.reshape(shaped),
        v_heads.reshape(shaped),
        segments,
        decay_rates,
        seg_before,
    )
    prefix = carried_in(
        (decay_total, kv_state),
        "seq",
        combine_states,
        (jnp.ones_like(decay_total), jnp.zeros_like(kv_state)),
    )
    incoming = prefix[1]
    steps_in = jnp.arange(seq_rows).astype(jnp.float32) + 1.0
    carry_in = jnp.where(
        (segments == seg_before)[None, :], jnp.exp(-decay_rates[:, None] * steps_in[None, :]), 0.0
    )
    wide_queries = q_heads.reshape(shaped).astype(jnp.float32)
    attended = (
        attended
        + jnp.einsum("thd,hde->the", wide_queries, incoming, precision=highest)
        * carry_in.T[:, :, None]
    )
    flat = attended.reshape(seq_rows, heads_dev * head_dim)
    power_sum = lax.psum(jnp.sum(flat * flat, axis=1), "tp")
    inv_rms = lax.rsqrt(power_sum / (heads_dev * head_dim * group_size) + 1e-06)
    normed = (flat * inv_rms[:, None] * norm_gain[None, :]).astype(jnp.bfloat16)
    return lax.psum_scatter(
        jnp.dot(normed, out_weight, preferred_element_type=jnp.float32)
        .astype(jnp.bfloat16)
        .astype(jnp.float32)
        .astype(jnp.bfloat16),
        "tp",
        scatter_dimension=0,
        tiled=True,
    )


def solution(mesh):
    return jax.shard_map(
        local,
        mesh=mesh,
        in_specs=(
            P(("seq", "tp"), None),
            P(("seq", "tp"), None),
            P(("seq", "tp"), None),
            P("tp"),
            P("tp"),
            P("tp", None),
            P(),
        ),
        out_specs=P(("seq", "tp"), None),
        check_vma=False,
    )
```

profile of v0, /device:TPU:0, one launch (start us, length us, event | category | flops | bytes accessed | tf_op | source)
XLA Modules:
  0.0 267.3 jit_solution(4730100146338197050)
XLA Ops:
  6.5 2.6 copy.76
  9.1 5.3 %all-to-all-start.2 = ((bf16[128,4,1536]{0,2,1:T(8,128)(2,1)}), bf16[128,4,1536]{0,2,1:T(8,128)(2,1)S(1)}, u32[]{:S(2)}, u32[]{:S(2)}) async-start(bf16[128,4,1536]{0,2,1:T(8,128)(2,1)} %bitcast.72), calls=%async_computation.2 | async-start | bytes 3145728 | tf_op jit(solution)/shard_map/all_to_all | solution.py:96
  15.4 2.6 copy.71
  20.1 13.6 %all-to-all-done.2 = bf16[128,4,1536]{0,2,1:T(8,128)(2,1)S(1)} async-done(((bf16[128,4,1536]{0,2,1:T(8,128)(2,1)}), bf16[128,4,1536]{0,2,1:T(8,128)(2,1)S(1)}, u32[]{:S(2)}, u32[]{:S(2)}) %all-to-all-start.2) | async-done | bytes 1572896 | tf_op jit(solution)/shard_map/all_to_all | solution.py:96
  33.7 4.5 %all-to-all-start.1 = ((bf16[128,4,1536]{0,2,1:T(8,128)(2,1)}), bf16[128,4,1536]{0,2,1:T(8,128)(2,1)}, u32[]{:S(2)}, u32[]{:S(2)}) async-start(bf16[128,4,1536]{0,2,1:T(8,128)(2,1)} %bitcast.69), calls=%async_computation.1 | async-start | bytes 3145728 | tf_op jit(solution)/shard_map/all_to_all | solution.py:95
  39.9 8.2 %copy.77 = bf16[4,128,1536]{1,0,2:T(4,128)(2,1)} copy(bf16[4,128,1536]{1,2,0:T(8,128)(2,1)S(1)} %bitcast.68) | data formatting | bytes 3145728 | tf_op jit(solution)/shard_map/all_to_all | solution.py:96
  48.1 3.8 %reshape_reshape.11 = bf16[2,256,12,128]{1,0,3,2:T(2,128)(2,1)S(1)} reshape(bf16[4,128,1536]{1,0,2:T(4,128)(2,1)} %copy.77) | data formatting | bytes 3145728 | tf_op jit(solution)/shard_map/reshape;reshape | solution.py:38
  51.9 2.8 %copy.78 = bf16[2,256,12,128]{3,1,2,0:T(8,128)(2,1)} copy(bf16[2,256,12,128]{1,0,3,2:T(2,128)(2,1)S(1)} %reshape_reshape.11) | data formatting | bytes 3145728 | tf_op jit(solution)/shard_map/reshape;reshape | solution.py:38
  56.9 8.5 %copy.72 = bf16[4,128,1536]{1,0,2:T(4,128)(2,1)} copy(bf16[4,128,1536]{1,2,0:T(8,128)(2,1)} %bitcast.3) | data formatting | bytes 3145728 | tf_op jit(solution)/shard_map/all_to_all | solution.py:95
  65.4 3.8 %reshape_reshape.10 = bf16[2,256,12,128]{1,0,3,2:T(2,128)(2,1)S(1)} reshape(bf16[4,128,1536]{1,0,2:T(4,128)(2,1)} %copy.72) | data formatting | bytes 3145728 | tf_op jit(solution)/shard_map/reshape;reshape | solution.py:37
  77.9 3.7 %all-to-all-start = ((bf16[128,4,1536]{0,2,1:T(8,128)(2,1)}), bf16[128,4,1536]{0,2,1:T(8,128)(2,1)S(1)}, u32[]{:S(2)}, u32[]{:S(2)}) async-start(bf16[128,4,1536]{0,2,1:T(8,128)(2,1)} %bitcast.71), calls=%async_computation | async-start | bytes 3145728 | tf_op jit(solution)/shard_map/all_to_all | solution.py:94
  86.4 13.8 %all-to-all-done = bf16[128,4,1536]{0,2,1:T(8,128)(2,1)S(1)} async-done(((bf16[128,4,1536]{0,2,1:T(8,128)(2,1)}), bf16[128,4,1536]{0,2,1:T(8,128)(2,1)S(1)}, u32[]{:S(2)}, u32[]{:S(2)}) %all-to-all-start) | async-done | bytes 1572896 | tf_op jit(solution)/shard_map/all_to_all | solution.py:94
  101.5 7.7 %copy.70 = bf16[4,128,1536]{1,0,2:T(4,128)(2,1)S(1)} copy(bf16[4,128,1536]{1,2,0:T(8,128)(2,1)} %bitcast.70) | data formatting | bytes 3145728 | tf_op jit(solution)/shard_map/all_to_all | solution.py:94
  109.1 2.3 reshape_reshape.9
  113.5 5.0 %copy.73 = bf16[2,256,12,128]{3,1,2,0:T(8,128)(2,1)} copy(bf16[2,256,12,128]{1,0,3,2:T(2,128)(2,1)} %reshape_reshape.9) | data formatting | bytes 3145728 | tf_op jit(solution)/shard_map/reshape;reshape | solution.py:36
  118.5 6.4 %fusion.3 = f32[2,12,256,128]{3,2,1,0:T(8,128)} fusion(bf16[2,256,12,128]{3,1,2,0:T(8,128)(2,1)} %copy.78, f32[12,256,256]{2,1,0:T(8,128)} %multiply_exponential_fusion, pred[2,256,256]{2,1,0:T(8,128)(4,1)S(1)} %compare_and_fusion, bf16[2,256,12,128]{3,1,2,0:T(8,128)(2,1)} %copy.73, bf16[2,256,12,128]{1,0,3,2:T(2,128)(2,1)S(1)} %copy-done.1), kind=kOutput, calls=%fused_computation.11 | convolution fusion | flops 810024960 | bytes 11141120 | tf_op jit(solution)/shard_map/bhts,bshd->bthd/dot_general | solution.py:48
  124.9 4.6 %fusion.7 = f32[2,256,12,128]{3,1,2,0:T(8,128)S(1)} fusion(f32[2,12,256,128]{3,2,1,0:T(8,128)} %fusion.3, f32[2,12,128,128]{3,2,1,0:T(8,128)} %get-tuple-element.133, bf16[2,256,12,128]{3,1,2,0:T(8,128)(2,1)} %copy.73, f32[2,256,12]{1,2,0:T(8,128)S(1)} %broadcast_select_fusion.1), kind=kOutput, calls=%fused_computation.18 | convolution fusion | flops 1209532416 | bytes 9461760 | tf_op jit(solution)/shard_map/bthd,bhde->bthe/dot_general | solution.py:80
  131.5 3.6 %copy.89 = f32[512,12,128]{0,2,1:T(8,128)} copy(f32[512,12,128]{2,0,1:T(8,128)} %bitcast.67) | data formatting | bytes 6291456 | tf_op jit(solution)/shard_map/reshape | solution.py:84
  135.3 16.0 %all-reduce = bf16[96]{0:T(256)(128)(2,1)S(1)} all-reduce(bf16[96]{0:T(256)(128)(2,1)S(1)} %dynamic-update-slice), channel_id=2, replica_groups=mesh['seq'=8,'tp'=4] {'seq'}, use_global_device_ids=true, to_apply=%add | all-reduce | flops 96 | bytes 384
  151.4 9.9 %while.30 = (s32[]{:T(128)}, f32[12,128,128]{2,1,0:T(8,128)S(1)}, s32[]{:T(128)}, bf16[8,12]{1,0:T(8,128)(2,1)S(1)}, bf16[8,12,128,128]{3,2,1,0:T(8,128)(2,1)}, /*index=5*/s32[]{:T(128)}, s32[]{:T(128)}) while((s32[]{:T(128)}, f32[12,128,128]{2,1,0:T(8,128)S(1)}, s32[]{:T(128)}, bf16[8,12]{1,0:T(8,128)(2,1)S(1)}, ...), condition=%wide.region_6.7_spmd.clone, body=%wide.region_5.6_spmd.clone.sunk | while | flops 983056 | bytes 1966313 | solution.py:23
  161.3 5.3 %multiply_reduce_fusion = (f32[512]{0:T(512)S(1)}, f32[512,12,128]{0,2,1:T(8,128)}) fusion(f32[512,12,128]{0,2,1:T(8,128)} %copy.89, f32[512,12]{0,1:T(8,128)S(1)} %exponential_select_fusion, f32[12,128,128]{2,1,0:T(8,128)S(1)} %get-tuple-element.136, bf16[512,12,128]{0,2,1:T(8,128)(2,1)S(1)} %copy-done.2), kind=kOutput, calls=%fused_computation.19 | convolution fusion | flops 1211104768 | bytes 8677376 | tf_op jit(solution)/shard_map/thd,hde->the/dot_general | solution.py:130
  166.7 8.2 %psum.7 = f32[512]{0:T(512)S(1)} all-reduce(f32[512]{0:T(512)S(1)} %get-tuple-element.208), channel_id=1, replica_groups=mesh['seq'=8,'tp'=4] {'tp'}, use_global_device_ids=true, to_apply=%region_8.9 | all-reduce | flops 512 | bytes 4096 | tf_op jit(solution)/shard_map/psum | solution.py:134
  177.1 15.7 %convolution_convert_fusion = bf16[512,6144]{1,0:T(8,128)(2,1)} fusion(bf16[512,1536]{0,1:T(8,128)(2,1)S(1)} %fusion.5, bf16[1536,6144]{1,0:T(8,128)(2,1)} %param.16), kind=kOutput, calls=%fused_computation.9 | convolution fusion | flops 9666822144 | bytes 26738688 | tf_op jit(solution)/shard_map/dot_general | solution.py:138
  192.8 67.6 %reduce-scatter.2.cloned.1.call-done = bf16[128,6144]{1,0:T(8,128)(2,1)} async-done(((bf16[512,6144]{1,0:T(8,128)(2,1)}), bf16[128,6144]{1,0:T(8,128)(2,1)}) %reduce-scatter.2.cloned.1.call-update) | async-done | bytes 1572880 | tf_op jit(solution)/shard_map/reduce_scatter | solution.py:137
  (92 shorter events, 39.5 us)
Async XLA Ops:
  9.1 5.3 %copy-start.7 = (s32[32]{0:T(128)S(1)}, s32[32]{0:T(128)}, u32[]{:S(2)}) copy-start(s32[32]{0:T(128)} %param.17) | copy-start | bytes 388
  9.1 24.5 %all-to-all-start.2 = ((bf16[128,4,1536]{0,2,1:T(8,128)(2,1)}), bf16[128,4,1536]{0,2,1:T(8,128)(2,1)S(1)}, u32[]{:S(2)}, u32[]{:S(2)}) async-start(bf16[128,4,1536]{0,2,1:T(8,128)(2,1)} %bitcast.72), calls=%async_computation.2 | async-start | bytes 3145728 | tf_op jit(solution)/shard_map/all_to_all | solution.py:96
  33.7 4.5 %copy-start.8 = (f32[12]{0:T(128)S(1)}, f32[12]{0:T(128)}, u32[]{:S(2)}) copy-start(f32[12]{0:T(128)} %param.14) | copy-start | bytes 148
  33.7 23.3 %all-to-all-start.1 = ((bf16[128,4,1536]{0,2,1:T(8,128)(2,1)}), bf16[128,4,1536]{0,2,1:T(8,128)(2,1)}, u32[]{:S(2)}, u32[]{:S(2)}) async-start(bf16[128,4,1536]{0,2,1:T(8,128)(2,1)} %bitcast.69), calls=%async_computation.1 | async-start | bytes 3145728 | tf_op jit(solution)/shard_map/all_to_all | solution.py:95
  38.1 113.3 %all-gather.4.cloned.1.call-start = ((), (), s32[]{:S(2)}) async-start(), calls=%async_computation.5 | async-start | bytes 3538944 | tf_op jit(solution)/shard_map/all_gather | solution.py:10
  69.2 1.2 copy-start
  70.4 1.5 copy-start.4
  74.7 1.6 copy-start.5
  77.9 4.0 %copy-start.9 = (u32[32]{0:T(128)S(1)}, u32[32]{0:T(128)}, u32[]{:S(2)}) copy-start(u32[32]{0:T(128)} %constant.69) | copy-start | bytes 388
  77.9 22.4 %all-to-all-start = ((bf16[128,4,1536]{0,2,1:T(8,128)(2,1)}), bf16[128,4,1536]{0,2,1:T(8,128)(2,1)S(1)}, u32[]{:S(2)}, u32[]{:S(2)}) async-start(bf16[128,4,1536]{0,2,1:T(8,128)(2,1)} %bitcast.71), calls=%async_computation | async-start | bytes 3145728 | tf_op jit(solution)/shard_map/all_to_all | solution.py:94
  81.6 178.9 %reduce-scatter.2.cloned.1.call-start = ((), (), s32[]{:S(2)}) async-start(), calls=%async_computation.4 | async-start | bytes 7864320 | tf_op jit(solution)/shard_map/reduce_scatter | solution.py:137
  100.2 1.2 copy-start.3
  113.5 5.0 %copy-start.1 = (bf16[2,256,12,128]{1,0,3,2:T(2,128)(2,1)S(1)}, bf16[2,256,12,128]{1,0,3,2:T(2,128)(2,1)}, u32[]{:S(2)}) copy-start(bf16[2,256,12,128]{1,0,3,2:T(2,128)(2,1)} %copy-done) | copy-start | bytes 4718596
  151.4 9.9 %copy-start.2 = (bf16[512,12,128]{0,2,1:T(8,128)(2,1)S(1)}, bf16[512,12,128]{0,2,1:T(8,128)(2,1)}, u32[]{:S(2)}) copy-start(bf16[512,12,128]{0,2,1:T(8,128)(2,1)} %reshape.308) | copy-start | bytes 4718596
  161.3 13.6 %copy-start.6 = (f32[1536]{0:T(1024)S(1)}, f32[1536]{0:T(1024)}, u32[]{:S(2)}) copy-start(f32[1536]{0:T(1024)} %param.15) | copy-start | bytes 18436
Sparse Core Ops, SparseCore 0:
  75.6 38.6 all-gather.3
  192.9 67.4 reduce-scatter.1
where the time goes:
time: 268 us; the launch traced here: 267 us
  waiting for transfers between devices  97.3 us (36%)
  local copies, waits for them, and re-layouts  61.4 us (23%)
  matrix products  32.6 us (12%)
  blocking collectives  24.2 us (9%)
  other arithmetic  23.5 us (9%)
  between operations  14.3 us (5%)
  starting transfers between devices  13.7 us (5%)
    reduce_scatter x1, waiting for transfers between devices, local(): lax.psum_scatter(jnp.dot(normed, out_weight, preferred_element_type=jnp.f...  67.6 us
    unnamed x1, blocking collectives  16 us
    dot_general x1, matrix products, local(): jnp.dot(normed, out_weight, preferred_element_type=jnp.float32)  15.7 us
    all_to_all x1, waiting for transfers between devices, local(): lax.all_to_all(queries, 'tp', split_axis=1, concat_axis=0, tiled=True)  13.8 us
    all_to_all x1, waiting for transfers between devices, local(): lax.all_to_all(values, 'tp', split_axis=1, concat_axis=0, tiled=True)  13.6 us
    unnamed x26, local copies, waits for them, and re-layouts  10.8 us
    select_n x8, other arithmetic, step(): return jax.tree.map(lambda a, b: jnp.where(reached, a, b), new, before)  9.55 us
    all_to_all x1, local copies, waits for them, and re-layouts, local(): lax.all_to_all(keys, 'tp', split_axis=1, concat_axis=0, tiled=True)  8.52 us
  transfers between devices with their start and end apart: 5, of which 4 were waited for; matrix products, arithmetic and copies ran while one was open for 23% of the time, Pallas kernels for 0%

commit v1 on v0

--- a/solution.py
+++ b/solution.py
@@ -1,6 +1,10 @@
+import functools
+
 import jax
 import jax.numpy as jnp
 from jax import lax
+from jax.experimental import pallas as pl
+from jax.experimental.pallas import tpu as pltpu
 from jax.sharding import PartitionSpec as P
 
 
@@ -144,10 +148,388 @@
         tiled=True,
     )
 
+MESH = pl.DeviceIdType.MESH
+FAR = 1e12
+BLOCK = 256
+HEAD_CHUNKS = 4
+COL_CHUNKS = 12
+
+
+def layer_kernel(
+    seq_count, rates, lengths, gain, q_in, k_in, v_in, w_in, out,
+    qb, kb, vb, wb, ab, dist, dist_end, dist_in, states, chain_in, chain_out, power,
+    pow_send, pow_recv, prod, first_in, second_out, second_in,
+    a2a_send, a2a_recv, own_sem, w_sem, chain_send, chain_recv, pow_ss, pow_rs, fs, fr, ss, sr,
+):
+    seq, me = lax.axis_index("seq"), lax.axis_index("tp")
+    x, y = lax.rem(me, 2), me // 2
+    peers = (y * 2 + (1 - x), (1 - y) * 2 + x, (1 - y) * 2 + (1 - x))
+    rows, width = q_in.shape[0], qb.shape[1]
+    group_rows = qb.shape[0]
+    heads = width // 128
+    chunk_heads = heads // HEAD_CHUNKS
+    chunk_cols = width // HEAD_CHUNKS
+    out_cols = out.shape[1] // COL_CHUNKS
+    blocks = group_rows // BLOCK
+    tensors = ((k_in, kb), (v_in, vb), (q_in, qb))
+
+    barrier = pltpu.get_barrier_semaphore()
+    for peer in peers:
+        pl.semaphore_signal(barrier, inc=1, device_id={"tp": peer}, device_id_type=MESH)
+
+    @pl.when(seq > 0)
+    def _():
+        pl.semaphore_signal(barrier, inc=1, device_id={"seq": seq - 1}, device_id_type=MESH)
+
+    @pl.when(seq < seq_count - 1)
+    def _():
+        pl.semaphore_signal(barrier, inc=1, device_id={"seq": seq + 1}, device_id_type=MESH)
+
+    def own_copy(i):
+        src, dst = tensors[i]
+        cols = pl.ds(pl.multiple_of(me * width, 128), width)
+        return pltpu.make_async_copy(
+            src.at[:, cols], dst.at[pl.ds(pl.multiple_of(me * rows, 128), rows)], own_sem.at[i]
+        )
+
+    for i in range(3):
+        own_copy(i).start()
+
+    before, after = (seq + seq_count - 1) // seq_count, (2 * seq_count - 2 - seq) // seq_count
+    pl.semaphore_wait(barrier, 3 + before + after)
+
+    def exchange(i, c, d):
+        src, dst = tensors[i]
+        peer = peers[d]
+        return pltpu.make_async_remote_copy(
+            src_ref=src.at[:, pl.ds(pl.multiple_of(peer * width + c * chunk_cols, 128), chunk_cols)],
+            dst_ref=dst.at[
+                pl.ds(pl.multiple_of(me * rows, 128), rows),
+                pl.ds(pl.multiple_of(c * chunk_cols, 128), chunk_cols),
+            ],
+            send_sem=a2a_send.at[i, c, d],
+            recv_sem=a2a_recv.at[i, c, d],
+            device_id={"tp": peer},
+            device_id_type=MESH,
+        )
+
+    def send_kv(c, _):
+        for i in (0, 1):
+            for d in (2, 0, 1):
+                exchange(i, c, d).start()
+        return 0
+
+    def send_q(c, _):
+        for d in (2, 0, 1):
+            exchange(2, c, d).start()
+        return 0
+
+    lax.fori_loop(0, HEAD_CHUNKS, send_kv, 0)
+    lax.fori_loop(0, HEAD_CHUNKS, send_q, 0)
+    load_w = pltpu.make_async_copy(w_in, wb, w_sem)
+    load_w.start()
+
+    first_row = seq * group_rows
+    ends, end = [], jnp.int32(0)
+    for j in range(lengths.shape[0]):
+        end = end + lengths[j]
+        ends.append(end)
+
+    def scalar_seg(position):
+        seg = jnp.int32(0)
+        for e in ends:
+            seg = seg + jnp.where(e <= position, 1, 0)
+        return seg
+
+    edge_segs = [scalar_seg(first_row - 1 + b * BLOCK) for b in range(blocks + 1)]
+    for b in range(blocks):
+        base = first_row + b * BLOCK
+        pos_c = lax.broadcasted_iota(jnp.int32, (BLOCK, 128), 0)
+        pos_r = lax.broadcasted_iota(jnp.int32, (8, BLOCK), 1)
+        seg_c, seg_r = jnp.zeros_like(pos_c), jnp.zeros_like(pos_r)
+        for e in ends:
+            seg_c = seg_c + jnp.where(e - base <= pos_c, 1, 0)
+            seg_r = seg_r + jnp.where(e - base <= pos_r, 1, 0)
+        steps = pos_c.astype(jnp.float32)
+        dist_end[b] = jnp.where(seg_c == edge_segs[b + 1], BLOCK - 1.0 - steps, FAR)
+        dist_in[b] = jnp.where(seg_c == edge_segs[b], steps + 1.0, FAR)
+        ti = lax.broadcasted_iota(jnp.int32, (BLOCK, BLOCK), 0)
+        si = lax.broadcasted_iota(jnp.int32, (BLOCK, BLOCK), 1)
+        same = jnp.concatenate([seg_c] * (BLOCK // 128), axis=1) == jnp.broadcast_to(
+            seg_r[:1], (BLOCK, BLOCK)
+        )
+        dist[b] = jnp.where(same & (ti >= si), (ti - si).astype(jnp.float32), FAR)
+    keep_dist = [
+        jnp.where(edge_segs[b + 1] == edge_segs[b], jnp.float32(BLOCK), jnp.float32(FAR))
+        for b in range(blocks)
+    ]
+
+    @pl.when(seq == 0)
+    def _():
+        chain_in[...] = jnp.zeros_like(chain_in)
+
+    def hop(c):
+        return pltpu.make_async_remote_copy(
+            src_ref=chain_out.at[c],
+            dst_ref=chain_in.at[c],
+            send_sem=chain_send.at[c],
+            recv_sem=chain_recv.at[c],
+            device_id={"seq": lax.rem(seq + 1, seq_count)},
+            device_id_type=MESH,
+        )
+
+    own_copy(0).wait()
+    own_copy(1).wait()
+
+    def state_chunk(c, _):
+        for i in (0, 1):
+            for d in range(3):
+                exchange(i, c, d).wait_recv()
+        for g in range(chunk_heads):
+            h = c * chunk_heads + g
+            cols = pl.ds(pl.multiple_of(h * 128, 128), 128)
+            rate = rates[h]
+            for b in range(blocks):
+                span = pl.ds(b * BLOCK, BLOCK)
+                weight = jnp.exp(dist_end[b] * -rate)
+                wk = (kb[span, cols].astype(jnp.float32) * weight).astype(jnp.bfloat16)
+                states[b, h] = lax.dot_general(
+                    wk, vb[span, cols], (((0,), (0,)), ((), ())), preferred_element_type=jnp.float32
+                )
+
+        @pl.when(seq > 0)
+        def _():
+            hop(c).wait_recv()
+
+        for g in range(chunk_heads):
+            h = c * chunk_heads + g
+            rate = rates[h]
+            entering = chain_in[c, g].astype(jnp.float32)
+            for b in range(blocks):
+                keep = jnp.exp(jnp.full((128, 128), keep_dist[b] * -rate, jnp.float32))
+                following = keep * entering + states[b, h]
+                states[b, h] = entering
+                entering = following
+            chain_out[c, g] = entering.astype(jnp.bfloat16)
+
+        @pl.when(seq < seq_count - 1)
+        def _():
+            hop(c).start()
+
+        return 0
+
+    lax.fori_loop(0, HEAD_CHUNKS, state_chunk, 0)
+
+    power[...] = jnp.zeros_like(power)
+    own_copy(2).wait()
+
+    def attend_chunk(c, _):
+        for d in range(3):
+            exchange(2, c, d).wait_recv()
+        for g in range(chunk_heads):
+            h = c * chunk_heads + g
+            cols = pl.ds(pl.multiple_of(h * 128, 128), 128)
+            rate = rates[h]
+            for b in range(blocks):
+                span = pl.ds(b * BLOCK, BLOCK)
+                q, k, v = qb[span, cols], kb[span, cols], vb[span, cols]
+                scores = lax.dot_general(
+                    q, k, (((1,), (1,)), ((), ())), preferred_element_type=jnp.float32
+                )
+                weighted = (scores * jnp.exp(dist[b] * -rate)).astype(jnp.bfloat16)
+                inside = jnp.dot(weighted, v, preferred_element_type=jnp.float32)
+                carried = jnp.dot(
+                    q, states[b, h].astype(jnp.bfloat16), preferred_element_type=jnp.float32
+                )
+                attended = inside + carried * jnp.exp(dist_in[b] * -rate)
+                power[span] += attended * attended
+                ab[span, cols] = (attended * gain[:, cols]).astype(jnp.bfloat16)
+        return 0
+
+    lax.fori_loop(0, HEAD_CHUNKS, attend_chunk, 0)
+    load_w.wait()
+
+    def ways(c):
+        odd = lax.rem(c, 2)
+        p1 = peers[0] * (1 - odd) + peers[1] * odd
+        p2 = peers[1] * (1 - odd) + peers[0] * odd
+        return p1, p2
+
+    def first_hop(c, which):
+        p1, _ = ways(c)
+        return pltpu.make_async_remote_copy(
+            src_ref=prod.at[c, p1 if which == 0 else peers[2]],
+            dst_ref=first_in.at[c, which],
+            send_sem=fs.at[c, which],
+            recv_sem=fr.at[c, which],
+            device_id={"tp": p1},
+            device_id_type=MESH,
+        )
+
+    def second_hop(c):
+        _, p2 = ways(c)
+        return pltpu.make_async_remote_copy(
+            src_ref=second_out.at[c],
+            dst_ref=second_in.at[c],
+            send_sem=ss.at[c],
+            recv_sem=sr.at[c],
+            device_id={"tp": p2},
+            device_id_type=MESH,
+        )
+
+    def pow_copy(d):
+        return pltpu.make_async_remote_copy(
+            src_ref=pow_send.at[peers[d]],
+            dst_ref=pow_recv.at[d],
+            send_sem=pow_ss.at[d],
+            recv_sem=pow_rs.at[d],
+            device_id={"tp": peers[d]},
+            device_id_type=MESH,
+        )
+
+    def project(c):
+        cols = pl.ds(pl.multiple_of(c * out_cols, 128), out_cols)
+        part = jnp.dot(ab[...], wb[:, cols], preferred_element_type=jnp.float32)
+        prod[c] = part.astype(jnp.bfloat16).reshape(prod.shape[1:])
+        first_hop(c, 1).start()
+        first_hop(c, 0).start()
+
+    def forward(c):
+        _, p2 = ways(c)
+        first_hop(c, 1).wait_recv()
+        second_out[c] = (
+            prod[c, p2].astype(jnp.float32) + first_in[c, 1].astype(jnp.float32)
+        ).astype(jnp.bfloat16)
+        second_hop(c).start()
+
+    lag = 3
+
+    def lead(c, _):
+        project(c)
+        return 0
+
+    def steady(c, _):
+        project(c)
+        forward(c - lag)
+        return 0
+
+    def trail(c, _):
+        forward(c)
+        return 0
+
+    lax.fori_loop(0, lag, lead, 0)
+    for j in range(4):
+        row = jnp.sum(power[pl.ds(j * rows, rows)].T, axis=0, keepdims=True)
+        pow_send[j] = jnp.broadcast_to(row, pow_send.shape[1:])
+    for d in range(3):
+        pow_copy(d).start()
+    lax.fori_loop(lag, COL_CHUNKS, steady, 0)
+    lax.fori_loop(COL_CHUNKS - lag, COL_CHUNKS, trail, 0)
+
+    total = pow_send[me]
+    for d in range(3):
+        pow_copy(d).wait_recv()
+        total = total + pow_recv[d]
+    scale = lax.rsqrt(total / (4 * width) + 1e-06)
+    scale = jnp.broadcast_to(scale[:1], (128, rows)).T
+    scale = jnp.concatenate([scale] * (out_cols // 128), axis=1)
+
+    def finish(c, _):
+        first_hop(c, 0).wait_recv()
+        second_hop(c).wait_recv()
+        summed = (
+            prod[c, me].astype(jnp.float32)
+            + first_in[c, 0].astype(jnp.float32)
+            + second_in[c].astype(jnp.float32)
+        )
+        cols = pl.ds(pl.multiple_of(c * out_cols, 128), out_cols)
+        out[:, cols] = (summed * scale).astype(jnp.bfloat16)
+        return 0
+
+    lax.fori_loop(0, COL_CHUNKS, finish, 0)
+
+    def drain_heads(c, _):
+        for i in range(3):
+            for d in range(3):
+                exchange(i, c, d).wait_send()
+
+        @pl.when(seq < seq_count - 1)
+        def _():
+            hop(c).wait_send()
+
+        return 0
+
+    def drain_cols(c, _):
+        first_hop(c, 0).wait_send()
+        first_hop(c, 1).wait_send()
+        second_hop(c).wait_send()
+        return 0
+
+    lax.fori_loop(0, HEAD_CHUNKS, drain_heads, 0)
+    lax.fori_loop(0, COL_CHUNKS, drain_cols, 0)
+    for d in range(3):
+        pow_copy(d).wait_send()
+
+
+def fused(queries, keys, values, decay_rates, norm_gain, out_weight, doc_lengths):
+    rows, model = queries.shape
+    width, out_width = out_weight.shape
+    heads = width // 128
+    group = rows * 4
+    blocks = group // BLOCK
+    per = heads // HEAD_CHUNKS
+    cols = out_width // COL_CHUNKS
+    bf16, f32 = jnp.bfloat16, jnp.float32
+    hbm, vmem = pl.BlockSpec(memory_space=pl.ANY), pl.BlockSpec(memory_space=pltpu.VMEM)
+    smem = pl.BlockSpec(memory_space=pltpu.SMEM)
+    dma = pltpu.SemaphoreType.DMA
+    return pl.pallas_call(
+        functools.partial(layer_kernel, lax.axis_size("seq")),
+        out_shape=jax.ShapeDtypeStruct((rows, out_width), bf16),
+        in_specs=[smem, smem, vmem, hbm, hbm, hbm, hbm],
+        out_specs=vmem,
+        scratch_shapes=[
+            pltpu.VMEM((group, width), bf16),
+            pltpu.VMEM((group, width), bf16),
+            pltpu.VMEM((group, width), bf16),
+            pltpu.VMEM((width, out_width), bf16),
+            pltpu.VMEM((group, width), bf16),
+            pltpu.VMEM((blocks, BLOCK, BLOCK), f32),
+            pltpu.VMEM((blocks, BLOCK, 128), f32),
+            pltpu.VMEM((blocks, BLOCK, 128), f32),
+            pltpu.VMEM((blocks, heads, 128, 128), f32),
+            pltpu.VMEM((HEAD_CHUNKS, per, 128, 128), bf16),
+            pltpu.VMEM((HEAD_CHUNKS, per, 128, 128), bf16),
+            pltpu.VMEM((group, 128), f32),
+            pltpu.VMEM((4, 8, rows), f32),
+            pltpu.VMEM((3, 8, rows), f32),
+            pltpu.VMEM((COL_CHUNKS, 4, rows, cols), bf16),
+            pltpu.VMEM((COL_CHUNKS, 2, rows, cols), bf16),
+            pltpu.VMEM((COL_CHUNKS, rows, cols), bf16),
+            pltpu.VMEM((COL_CHUNKS, rows, cols), bf16),
+            dma((3, HEAD_CHUNKS, 3)),
+            dma((3, HEAD_CHUNKS, 3)),
+            dma((3,)),
+            dma,
+            dma((HEAD_CHUNKS,)),
+            dma((HEAD_CHUNKS,)),
+            dma((3,)),
+            dma((3,)),
+            dma((COL_CHUNKS, 2)),
+            dma((COL_CHUNKS, 2)),
+            dma((COL_CHUNKS,)),
+            dma((COL_CHUNKS,)),
+        ],
+        compiler_params=pltpu.CompilerParams(
+            collective_id=0, has_side_effects=True, vmem_limit_bytes=58 * 2**20
+        ),
+        name="layer",
+    )(decay_rates, doc_lengths, norm_gain.reshape(1, width), queries, keys, values, out_weight)
+
 
 def solution(mesh):
     return jax.shard_map(
-        local,
+        fused if mesh.shape["tp"] == 4 else local,
         mesh=mesh,
         in_specs=(
             P(("seq", "tp"), None),

time: 268 us -> 120 us (0.45)
  Pallas kernels: 0 us -> 116 us
  waiting for transfers between devices: 97.3 us -> 0 us
  local copies, waits for them, and re-layouts: 61.4 us -> 3.98 us
  matrix products: 32.6 us -> 0 us
  blocking collectives: 24.2 us -> 0 us
  other arithmetic: 23.5 us -> 0 us
  between operations: 14.3 us -> 0.01 us
  starting transfers between devices: 13.7 us -> 0 us
    pallas_call x0 -> x1, Pallas kernels: none -> 116 us  [fused(): pl.pallas_call(functools.partial(layer_kernel, lax.axis_size('seq')), out...]
    reduce_scatter x1 -> x0, waiting for transfers between devices: 67.6 us -> none  [local(): lax.psum_scatter(jnp.dot(normed, out_weight, preferred_element_type=jnp.f...]
    dot_general x5 -> x0, matrix products: 32.6 us -> none  [the longest x1 15.7 us: local(): jnp.dot(normed, out_weight, preferred_element_type=jnp.float32)]
    all_to_all x3 -> x0, waiting for transfers between devices: 29.6 us -> none  [the longest x1 13.8 us: local(): lax.all_to_all(queries, 'tp', split_axis=1, concat_axis=0, tiled=True)]
    all_to_all x3 -> x0, local copies, waits for them, and re-layouts: 24.3 us -> none  [the longest x1 8.52 us: local(): lax.all_to_all(keys, 'tp', split_axis=1, concat_axis=0, tiled=True)]
    another operation x5 -> x0, local copies, waits for them, and re-layouts: 17.7 us -> none  [the longest x2 7.34 us: local_pass(): q_blocks = q_heads.reshape(shape_four)]
    unnamed x1 -> x0, blocking collectives: 16 us -> none
    all_to_all x3 -> x0, starting transfers between devices: 13.5 us -> none  [the longest x1 5.29 us: local(): lax.all_to_all(values, 'tp', split_axis=1, concat_axis=0, tiled=True)]
  transfers between devices with their start and end apart: 5 -> 0, of which waited for: 4 -> 0; matrix products, arithmetic and copies ran while one was open for 23% -> 0% of each run, Pallas kernels for 0% -> 0%
where the time goes in v1:
time: 120 us
  Pallas kernels  116 us (97%)
  local copies, waits for them, and re-layouts  3.98 us (3%)
    pallas_call x1, Pallas kernels, fused(): pl.pallas_call(functools.partial(layer_kernel, lax.axis_size('seq')), out...  116 us
    unnamed x1, local copies, waits for them, and re-layouts  2.69 us

profile of v1, /device:TPU:0, one launch (start us, length us, event | category | flops | bytes accessed | tf_op | source)
XLA Modules:
  0.0 119.8 jit_solution(12169532396038982997)
XLA Ops:
  0.0 1.3 %reshape.3.gain = f32[1,1536]{1,0:T(1,128)} reshape(f32[1536]{0:T(1024)} %param.11) | data formatting | bytes 12288 | tf_op jit(solution)/shard_map/reshape | solution.py:527
  1.3 115.8 %layer.1 = bf16[128,6144]{1,0:T(8,128)(2,1)} custom-call(f32[12]{0:T(128)} %rates.1, s32[32]{0:T(128)} %lengths.1, f32[1,1536]{1,0:T(1,128)} %reshape.3.gain, bf16[128,6144]{1,0:T(8,128)(2,1)} %q_in.1, bf16[128,6144]{1,0:T(8,128)(2,1)} %k_in.1, bf16[128,6144]{1,0:T(8,128)(2,1)} %v_in.1, bf16[1536,6144]{1,0:T(8,128)(2,1)} %w_in.1), custom_call_target="tpu_custom_call" | custom-call | tf_op jit(solution)/shard_map/layer/pallas_call | solution.py:486
  117.1 2.7 %copy.9 = bf16[128,6144]{1,0:T(8,128)(2,1)} copy(bf16[128,6144]{1,0:T(8,128)(2,1)} %layer.1) | data formatting | bytes 3145728

commit v2 on v1

--- a/solution.py
+++ b/solution.py
@@ -153,6 +153,7 @@
 BLOCK = 256
 HEAD_CHUNKS = 4
 COL_CHUNKS = 12
+LAG = 4
 
 
 def layer_kernel(
@@ -343,7 +344,7 @@
                 )
                 attended = inside + carried * jnp.exp(dist_in[b] * -rate)
                 power[span] += attended * attended
-                ab[span, cols] = (attended * gain[:, cols]).astype(jnp.bfloat16)
+                ab[span, cols] = (attended * gain[cols]).astype(jnp.bfloat16)
         return 0
 
     lax.fori_loop(0, HEAD_CHUNKS, attend_chunk, 0)
@@ -392,7 +393,6 @@
         part = jnp.dot(ab[...], wb[:, cols], preferred_element_type=jnp.float32)
         prod[c] = part.astype(jnp.bfloat16).reshape(prod.shape[1:])
         first_hop(c, 1).start()
-        first_hop(c, 0).start()
 
     def forward(c):
         _, p2 = ways(c)
@@ -401,8 +401,9 @@
             prod[c, p2].astype(jnp.float32) + first_in[c, 1].astype(jnp.float32)
         ).astype(jnp.bfloat16)
         second_hop(c).start()
-
-    lag = 3
+        first_hop(c, 0).start()
+
+    lag = LAG
 
     def lead(c, _):
         project(c)
@@ -524,7 +525,7 @@
             collective_id=0, has_side_effects=True, vmem_limit_bytes=58 * 2**20
         ),
         name="layer",
-    )(decay_rates, doc_lengths, norm_gain.reshape(1, width), queries, keys, values, out_weight)
+    )(decay_rates, doc_lengths, norm_gain, queries, keys, values, out_weight)
 
 
 def solution(mesh):

time: 120 us -> 119 us (level)
  local copies, waits for them, and re-layouts: 3.98 us -> 2.69 us
    reshape x1 -> x0, local copies, waits for them, and re-layouts: 1.29 us -> none  [fused(): norm_gain.reshape(1, width)]
where the time goes in v2:
time: 119 us; the launch traced here: 118 us
  Pallas kernels  116 us (97%)
  local copies, waits for them, and re-layouts  2.69 us (2%)
    pallas_call x1, Pallas kernels, fused(): pl.pallas_call(functools.partial(layer_kernel, lax.axis_size('seq')), out...  116 us
    unnamed x1, local copies, waits for them, and re-layouts  2.69 us

profile of v2, /device:TPU:0, one launch (start us, length us, event | category | flops | bytes accessed | tf_op | source)
XLA Modules:
  0.0 118.4 jit_solution(18392136069669855933)
XLA Ops:
  0.0 115.7 %layer.1 = bf16[128,6144]{1,0:T(8,128)(2,1)} custom-call(f32[12]{0:T(128)} %rates.1, s32[32]{0:T(128)} %lengths.1, f32[1536]{0:T(1024)} %gain.1, bf16[128,6144]{1,0:T(8,128)(2,1)} %q_in.1, bf16[128,6144]{1,0:T(8,128)(2,1)} %k_in.1, bf16[128,6144]{1,0:T(8,128)(2,1)} %v_in.1, bf16[1536,6144]{1,0:T(8,128)(2,1)} %w_in.1), custom_call_target="tpu_custom_call" | custom-call | tf_op jit(solution)/shard_map/layer/pallas_call | solution.py:487
  115.7 2.7 %copy.9 = bf16[128,6144]{1,0:T(8,128)(2,1)} copy(bf16[128,6144]{1,0:T(8,128)(2,1)} %layer.1) | data formatting | bytes 3145728

commit v3 on v2

--- a/solution.py
+++ b/solution.py
@@ -153,26 +153,27 @@
 BLOCK = 256
 HEAD_CHUNKS = 4
 COL_CHUNKS = 12
-LAG = 4
+HALVES = 2
 
 
 def layer_kernel(
     seq_count, rates, lengths, gain, q_in, k_in, v_in, w_in, out,
     qb, kb, vb, wb, ab, dist, dist_end, dist_in, states, chain_in, chain_out, power,
-    pow_send, pow_recv, prod, first_in, second_out, second_in,
-    a2a_send, a2a_recv, own_sem, w_sem, chain_send, chain_recv, pow_ss, pow_rs, fs, fr, ss, sr,
+    pow_send, pow_recv, scale_rows, prod, first_in, second_out, second_in,
+    a2a_send, a2a_recv, q_send, q_recv, own_sem, w_sem, chain_send, chain_recv, pow_ss, pow_rs, fs, fr, ss, sr,
 ):
     seq, me = lax.axis_index("seq"), lax.axis_index("tp")
     x, y = lax.rem(me, 2), me // 2
     peers = (y * 2 + (1 - x), (1 - y) * 2 + x, (1 - y) * 2 + (1 - x))
-    rows, width = q_in.shape[0], qb.shape[1]
-    group_rows = qb.shape[0]
+    rows, width = q_in.shape[0], kb.shape[1]
+    group_rows = kb.shape[0]
+    half_rows, half_block = rows // HALVES, BLOCK // HALVES
     heads = width // 128
     chunk_heads = heads // HEAD_CHUNKS
     chunk_cols = width // HEAD_CHUNKS
     out_cols = out.shape[1] // COL_CHUNKS
     blocks = group_rows // BLOCK
-    tensors = ((k_in, kb), (v_in, vb), (q_in, qb))
+    tensors = ((k_in, kb), (v_in, vb))
 
     barrier = pltpu.get_barrier_semaphore()
     for peer in peers:
@@ -193,8 +194,17 @@
             src.at[:, cols], dst.at[pl.ds(pl.multiple_of(me * rows, 128), rows)], own_sem.at[i]
         )
 
-    for i in range(3):
+    def own_q(r):
+        return pltpu.make_async_copy(
+            q_in.at[pl.ds(r * half_rows, half_rows), pl.ds(pl.multiple_of(me * width, 128), width)],
+            qb.at[r, pl.ds(pl.multiple_of(me * half_rows, half_rows), half_rows)],
+            own_sem.at[2 + r],
+        )
+
+    for i in range(2):
         own_copy(i).start()
+    for r in range(HALVES):
+        own_q(r).start()
 
     before, after = (seq + seq_count - 1) // seq_count, (2 * seq_count - 2 - seq) // seq_count
     pl.semaphore_wait(barrier, 3 + before + after)
@@ -220,13 +230,23 @@
                 exchange(i, c, d).start()
         return 0
 
-    def send_q(c, _):
+    def exchange_q(r, d):
+        peer = peers[d]
+        return pltpu.make_async_remote_copy(
+            src_ref=q_in.at[
+                pl.ds(r * half_rows, half_rows), pl.ds(pl.multiple_of(peer * width, 128), width)
+            ],
+            dst_ref=qb.at[r, pl.ds(pl.multiple_of(me * half_rows, half_rows), half_rows)],
+            send_sem=q_send.at[r, d],
+            recv_sem=q_recv.at[r, d],
+            device_id={"tp": peer},
+            device_id_type=MESH,
+        )
+
+    lax.fori_loop(0, HEAD_CHUNKS, send_kv, 0)
+    for r in range(HALVES):
         for d in (2, 0, 1):
-            exchange(2, c, d).start()
-        return 0
-
-    lax.fori_loop(0, HEAD_CHUNKS, send_kv, 0)
-    lax.fori_loop(0, HEAD_CHUNKS, send_q, 0)
+            exchange_q(r, d).start()
     load_w = pltpu.make_async_copy(w_in, wb, w_sem)
     load_w.start()
 
@@ -245,21 +265,33 @@
     edge_segs = [scalar_seg(first_row - 1 + b * BLOCK) for b in range(blocks + 1)]
     for b in range(blocks):
         base = first_row + b * BLOCK
-        pos_c = lax.broadcasted_iota(jnp.int32, (BLOCK, 128), 0)
+        pos_k = lax.broadcasted_iota(jnp.int32, (BLOCK, 128), 0)
         pos_r = lax.broadcasted_iota(jnp.int32, (8, BLOCK), 1)
-        seg_c, seg_r = jnp.zeros_like(pos_c), jnp.zeros_like(pos_r)
-        for e in ends:
-            seg_c = seg_c + jnp.where(e - base <= pos_c, 1, 0)
-            seg_r = seg_r + jnp.where(e - base <= pos_r, 1, 0)
-        steps = pos_c.astype(jnp.float32)
-        dist_end[b] = jnp.where(seg_c == edge_segs[b + 1], BLOCK - 1.0 - steps, FAR)
-        dist_in[b] = jnp.where(seg_c == edge_segs[b], steps + 1.0, FAR)
-        ti = lax.broadcasted_iota(jnp.int32, (BLOCK, BLOCK), 0)
-        si = lax.broadcasted_iota(jnp.int32, (BLOCK, BLOCK), 1)
-        same = jnp.concatenate([seg_c] * (BLOCK // 128), axis=1) == jnp.broadcast_to(
-            seg_r[:1], (BLOCK, BLOCK)
-        )
-        dist[b] = jnp.where(same & (ti >= si), (ti - si).astype(jnp.float32), FAR)
+
+        def segs(pos):
+            seg = jnp.zeros_like(pos)
+            for e in ends:
+                seg = seg + jnp.where(e - base <= pos, 1, 0)
+            return seg
+
+        seg_r = segs(pos_r)
+        dist_end[b] = jnp.where(
+            segs(pos_k) == edge_segs[b + 1], BLOCK - 1.0 - pos_k.astype(jnp.float32), FAR
+        )
+        for r in range(HALVES):
+            at = lax.broadcasted_iota(jnp.int32, (half_block, 128), 0)
+            pos_q = at + r * half_rows
+            for edge in range(half_rows, half_block, half_rows):
+                pos_q = pos_q + jnp.where(at >= edge, rows - half_rows, 0)
+            seg_q = segs(pos_q)
+            dist_in[r, b] = jnp.where(
+                seg_q == edge_segs[b], pos_q.astype(jnp.float32) + 1.0, FAR
+            )
+            wide_seg = jnp.concatenate([seg_q] * (BLOCK // 128), axis=1)
+            wide_pos = jnp.concatenate([pos_q] * (BLOCK // 128), axis=1)
+            gap = wide_pos - lax.broadcasted_iota(jnp.int32, (half_block, BLOCK), 1)
+            same = wide_seg == jnp.broadcast_to(seg_r[:1], (half_block, BLOCK))
+            dist[r, b] = jnp.where(same & (gap >= 0), gap.astype(jnp.float32), FAR)
     keep_dist = [
         jnp.where(edge_segs[b + 1] == edge_segs[b], jnp.float32(BLOCK), jnp.float32(FAR))
         for b in range(blocks)
@@ -322,32 +354,36 @@
     lax.fori_loop(0, HEAD_CHUNKS, state_chunk, 0)
 
     power[...] = jnp.zeros_like(power)
-    own_copy(2).wait()
-
-    def attend_chunk(c, _):
+
+    def attend(r):
+        own_q(r).wait()
         for d in range(3):
-            exchange(2, c, d).wait_recv()
-        for g in range(chunk_heads):
-            h = c * chunk_heads + g
-            cols = pl.ds(pl.multiple_of(h * 128, 128), 128)
-            rate = rates[h]
-            for b in range(blocks):
-                span = pl.ds(b * BLOCK, BLOCK)
-                q, k, v = qb[span, cols], kb[span, cols], vb[span, cols]
-                scores = lax.dot_general(
-                    q, k, (((1,), (1,)), ((), ())), preferred_element_type=jnp.float32
-                )
-                weighted = (scores * jnp.exp(dist[b] * -rate)).astype(jnp.bfloat16)
-                inside = jnp.dot(weighted, v, preferred_element_type=jnp.float32)
-                carried = jnp.dot(
-                    q, states[b, h].astype(jnp.bfloat16), preferred_element_type=jnp.float32
-                )
-                attended = inside + carried * jnp.exp(dist_in[b] * -rate)
-                power[span] += attended * attended
-                ab[span, cols] = (attended * gain[cols]).astype(jnp.bfloat16)
-        return 0
-
-    lax.fori_loop(0, HEAD_CHUNKS, attend_chunk, 0)
+            exchange_q(r, d).wait_recv()
+
+        def attend_chunk(c, _):
+            for g in range(chunk_heads):
+                h = c * chunk_heads + g
+                cols = pl.ds(pl.multiple_of(h * 128, 128), 128)
+                rate = rates[h]
+                for b in range(blocks):
+                    span, mine = pl.ds(b * BLOCK, BLOCK), pl.ds(b * half_block, half_block)
+                    q, k, v = qb[r, mine, cols], kb[span, cols], vb[span, cols]
+                    scores = lax.dot_general(
+                        q, k, (((1,), (1,)), ((), ())), preferred_element_type=jnp.float32
+                    )
+                    weighted = (scores * jnp.exp(dist[r, b] * -rate)).astype(jnp.bfloat16)
+                    inside = jnp.dot(weighted, v, preferred_element_type=jnp.float32)
+                    carried = jnp.dot(
+                        q, states[b, h].astype(jnp.bfloat16), preferred_element_type=jnp.float32
+                    )
+                    attended = inside + carried * jnp.exp(dist_in[r, b] * -rate)
+                    power[r, mine] += attended * attended
+                    ab[r, mine, cols] = (attended * gain[cols]).astype(jnp.bfloat16)
+            return 0
+
+        lax.fori_loop(0, HEAD_CHUNKS, attend_chunk, 0)
+
+    attend(0)
     load_w.wait()
 
     def ways(c):
@@ -389,8 +425,8 @@
         )
 
     def project(c):
-        cols = pl.ds(pl.multiple_of(c * out_cols, 128), out_cols)
-        part = jnp.dot(ab[...], wb[:, cols], preferred_element_type=jnp.float32)
+        cols = pl.ds(pl.multiple_of(lax.rem(c, COL_CHUNKS) * out_cols, 128), out_cols)
+        part = jnp.dot(ab[c // COL_CHUNKS], wb[:, cols], preferred_element_type=jnp.float32)
         prod[c] = part.astype(jnp.bfloat16).reshape(prod.shape[1:])
         first_hop(c, 1).start()
 
@@ -403,7 +439,18 @@
         second_hop(c).start()
         first_hop(c, 0).start()
 
-    lag = LAG
+    def finish(c):
+        first_hop(c, 0).wait_recv()
+        second_hop(c).wait_recv()
+        summed = (
+            prod[c, me].astype(jnp.float32)
+            + first_in[c, 0].astype(jnp.float32)
+            + second_in[c].astype(jnp.float32)
+        )
+        r = c // COL_CHUNKS
+        cols = pl.ds(pl.multiple_of(lax.rem(c, COL_CHUNKS) * out_cols, 128), out_cols)
+        span = pl.ds(pl.multiple_of(r * half_rows, half_rows), half_rows)
+        out[span, cols] = (summed * scale_rows[r]).astype(jnp.bfloat16)
 
     def lead(c, _):
         project(c)
@@ -411,21 +458,28 @@
 
     def steady(c, _):
         project(c)
-        forward(c - lag)
+        forward(c - COL_CHUNKS)
         return 0
 
     def trail(c, _):
         forward(c)
-        return 0
-
-    lax.fori_loop(0, lag, lead, 0)
+        finish(c - COL_CHUNKS)
+        return 0
+
+    def last(c, _):
+        finish(c)
+        return 0
+
+    units = HALVES * COL_CHUNKS
+    lax.fori_loop(0, COL_CHUNKS, lead, 0)
+    attend(1)
     for j in range(4):
-        row = jnp.sum(power[pl.ds(j * rows, rows)].T, axis=0, keepdims=True)
+        own_rows = [power[r, pl.ds(j * half_rows, half_rows)] for r in range(HALVES)]
+        row = jnp.sum(jnp.concatenate(own_rows, axis=0).T, axis=0, keepdims=True)
         pow_send[j] = jnp.broadcast_to(row, pow_send.shape[1:])
     for d in range(3):
         pow_copy(d).start()
-    lax.fori_loop(lag, COL_CHUNKS, steady, 0)
-    lax.fori_loop(COL_CHUNKS - lag, COL_CHUNKS, trail, 0)
+    lax.fori_loop(COL_CHUNKS, units, steady, 0)
 
     total = pow_send[me]
     for d in range(3):
@@ -433,24 +487,15 @@
         total = total + pow_recv[d]
     scale = lax.rsqrt(total / (4 * width) + 1e-06)
     scale = jnp.broadcast_to(scale[:1], (128, rows)).T
-    scale = jnp.concatenate([scale] * (out_cols // 128), axis=1)
-
-    def finish(c, _):
-        first_hop(c, 0).wait_recv()
-        second_hop(c).wait_recv()
-        summed = (
-            prod[c, me].astype(jnp.float32)
-            + first_in[c, 0].astype(jnp.float32)
-            + second_in[c].astype(jnp.float32)
-        )
-        cols = pl.ds(pl.multiple_of(c * out_cols, 128), out_cols)
-        out[:, cols] = (summed * scale).astype(jnp.bfloat16)
-        return 0
-
-    lax.fori_loop(0, COL_CHUNKS, finish, 0)
+    for r in range(HALVES):
+        part = scale[r * half_rows : (r + 1) * half_rows]
+        scale_rows[r] = jnp.concatenate([part] * (out_cols // 128), axis=1)
+
+    lax.fori_loop(COL_CHUNKS, units, trail, 0)
+    lax.fori_loop(COL_CHUNKS, units, last, 0)
 
     def drain_heads(c, _):
-        for i in range(3):
+        for i in range(2):
             for d in range(3):
                 exchange(i, c, d).wait_send()
 
@@ -467,7 +512,10 @@
         return 0
 
     lax.fori_loop(0, HEAD_CHUNKS, drain_heads, 0)
-    lax.fori_loop(0, COL_CHUNKS, drain_cols, 0)
+    lax.fori_loop(0, units, drain_cols, 0)
+    for r in range(HALVES):
+        for d in range(3):
+            exchange_q(r, d).wait_send()
     for d in range(3):
         pow_copy(d).wait_send()
 
@@ -480,6 +528,7 @@
     blocks = group // BLOCK
     per = heads // HEAD_CHUNKS
     cols = out_width // COL_CHUNKS
+    units, half = HALVES * COL_CHUNKS, rows // HALVES
     bf16, f32 = jnp.bfloat16, jnp.float32
     hbm, vmem = pl.BlockSpec(memory_space=pl.ANY), pl.BlockSpec(memory_space=pltpu.VMEM)
     smem = pl.BlockSpec(memory_space=pltpu.SMEM)
@@ -490,36 +539,39 @@
         in_specs=[smem, smem, vmem, hbm, hbm, hbm, hbm],
         out_specs=vmem,
         scratch_shapes=[
-            pltpu.VMEM((group, width), bf16),
+            pltpu.VMEM((HALVES, group // HALVES, width), bf16),
             pltpu.VMEM((group, width), bf16),
             pltpu.VMEM((group, width), bf16),
             pltpu.VMEM((width, out_width), bf16),
-            pltpu.VMEM((group, width), bf16),
-            pltpu.VMEM((blocks, BLOCK, BLOCK), f32),
+            pltpu.VMEM((HALVES, group // HALVES, width), bf16),
+            pltpu.VMEM((HALVES, blocks, BLOCK // HALVES, BLOCK), f32),
             pltpu.VMEM((blocks, BLOCK, 128), f32),
-            pltpu.VMEM((blocks, BLOCK, 128), f32),
+            pltpu.VMEM((HALVES, blocks, BLOCK // HALVES, 128), f32),
             pltpu.VMEM((blocks, heads, 128, 128), f32),
             pltpu.VMEM((HEAD_CHUNKS, per, 128, 128), bf16),
             pltpu.VMEM((HEAD_CHUNKS, per, 128, 128), bf16),
-            pltpu.VMEM((group, 128), f32),
+            pltpu.VMEM((HALVES, group // HALVES, 128), f32),
             pltpu.VMEM((4, 8, rows), f32),
             pltpu.VMEM((3, 8, rows), f32),
-            pltpu.VMEM((COL_CHUNKS, 4, rows, cols), bf16),
-            pltpu.VMEM((COL_CHUNKS, 2, rows, cols), bf16),
-            pltpu.VMEM((COL_CHUNKS, rows, cols), bf16),
-            pltpu.VMEM((COL_CHUNKS, rows, cols), bf16),
-            dma((3, HEAD_CHUNKS, 3)),
-            dma((3, HEAD_CHUNKS, 3)),
-            dma((3,)),
+            pltpu.VMEM((HALVES, half, cols), f32),
+            pltpu.VMEM((units, 4, half, cols), bf16),
+            pltpu.VMEM((units, 2, half, cols), bf16),
+            pltpu.VMEM((units, half, cols), bf16),
+            pltpu.VMEM((units, half, cols), bf16),
+            dma((2, HEAD_CHUNKS, 3)),
+            dma((2, HEAD_CHUNKS, 3)),
+            dma((HALVES, 3)),
+            dma((HALVES, 3)),
+            dma((2 + HALVES,)),
             dma,
             dma((HEAD_CHUNKS,)),
             dma((HEAD_CHUNKS,)),
             dma((3,)),
             dma((3,)),
-            dma((COL_CHUNKS, 2)),
-            dma((COL_CHUNKS, 2)),
-            dma((COL_CHUNKS,)),
-            dma((COL_CHUNKS,)),
+            dma((units, 2)),
+            dma((units, 2)),
+            dma((units,)),
+            dma((units,)),
         ],
         compiler_params=pltpu.CompilerParams(
             collective_id=0, has_side_effects=True, vmem_limit_bytes=58 * 2**20

time: 119 us -> 116 us (0.975)
  Pallas kernels: 116 us -> 112 us
    pallas_call x1, Pallas kernels: 116 us -> 112 us  [fused(): pl.pallas_call(functools.partial(layer_kernel, lax.axis_size('seq')), out...]
where the time goes in v3:
time: 116 us; the launch traced here: 114 us
  Pallas kernels  112 us (97%)
  local copies, waits for them, and re-layouts  2.69 us (2%)
    pallas_call x1, Pallas kernels, fused(): pl.pallas_call(functools.partial(layer_kernel, lax.axis_size('seq')), out...  112 us
    unnamed x1, local copies, waits for them, and re-layouts  2.69 us

profile of v3, /device:TPU:0, one launch (start us, length us, event | category | flops | bytes accessed | tf_op | source)
XLA Modules:
  0.0 114.3 jit_solution(9692941099391158472)
XLA Ops:
  0.0 111.6 %layer.1 = bf16[128,6144]{1,0:T(8,128)(2,1)} custom-call(f32[12]{0:T(128)} %rates.1, s32[32]{0:T(128)} %lengths.1, f32[1536]{0:T(1024)} %gain.1, bf16[128,6144]{1,0:T(8,128)(2,1)} %q_in.1, bf16[128,6144]{1,0:T(8,128)(2,1)} %k_in.1, bf16[128,6144]{1,0:T(8,128)(2,1)} %v_in.1, bf16[1536,6144]{1,0:T(8,128)(2,1)} %w_in.1), custom_call_target="tpu_custom_call" | custom-call | tf_op jit(solution)/shard_map/layer/pallas_call | solution.py:536
  111.6 2.7 %copy.9 = bf16[128,6144]{1,0:T(8,128)(2,1)} copy(bf16[128,6144]{1,0:T(8,128)(2,1)} %layer.1) | data formatting | bytes 3145728

commit v4 on v3

--- a/solution.py
+++ b/solution.py
@@ -152,7 +152,7 @@
 FAR = 1e12
 BLOCK = 256
 HEAD_CHUNKS = 4
-COL_CHUNKS = 12
+COL_CHUNKS = 6
 HALVES = 2
 
 

time: 116 us -> 115 us (level)
  no operation moved by 1% of the time
where the time goes in v4:
time: 115 us; the launch traced here: 114 us
  Pallas kernels  111 us (97%)
  local copies, waits for them, and re-layouts  2.69 us (2%)
    pallas_call x1, Pallas kernels, fused(): pl.pallas_call(functools.partial(layer_kernel, lax.axis_size('seq')), out...  111 us
    unnamed x1, local copies, waits for them, and re-layouts  2.69 us

profile of v4, /device:TPU:0, one launch (start us, length us, event | category | flops | bytes accessed | tf_op | source)
XLA Modules:
  0.0 113.6 jit_solution(13886538731316179070)
XLA Ops:
  0.0 110.9 %layer.1 = bf16[128,6144]{1,0:T(8,128)(2,1)} custom-call(f32[12]{0:T(128)} %rates.1, s32[32]{0:T(128)} %lengths.1, f32[1536]{0:T(1024)} %gain.1, bf16[128,6144]{1,0:T(8,128)(2,1)} %q_in.1, bf16[128,6144]{1,0:T(8,128)(2,1)} %k_in.1, bf16[128,6144]{1,0:T(8,128)(2,1)} %v_in.1, bf16[1536,6144]{1,0:T(8,128)(2,1)} %w_in.1), custom_call_target="tpu_custom_call" | custom-call | tf_op jit(solution)/shard_map/layer/pallas_call | solution.py:536
  110.9 2.7 %copy.9 = bf16[128,6144]{1,0:T(8,128)(2,1)} copy(bf16[128,6144]{1,0:T(8,128)(2,1)} %layer.1) | data formatting | bytes 3145728
